TPU v7x, 32 devices: a whole 2x2x4 slice. The times are simulated.
32 devices in a mesh: frames: 2 (over y), wide: 4 (over z), narrow: 4 (over x, core).
Axes of the slice: x: 2, y: 2, z: 4, core: 2. Of those that a mesh axis runs over, the one named last changes fastest.
Arguments:
- slc: bfloat16 [2, 16, 80, 5120], P(None, ('frames', 'wide'), 'narrow'), parts along dimension 1, may hold values from -6 to 6
- pair_list: int32 [16, 2], replicated, may hold values from 0 to 7, as said below
- owner: int32 [16], replicated, may hold values from 0 to 15, each once
Outputs:
- interferogram: float32 [2, 32, 16, 256], P(None, ('frames', 'wide'), 'narrow'), parts along dimension 1
- coherence: float32 [32, 16, 256], P(('frames', 'wide'), 'narrow'), parts along dimension 0
There are 2 independent parts, one for each index of `frames`. A program takes and returns all parts, laid end to end along the dimension named above; an argument that names none is the same for every part. Nothing has to cross between parts.
Inputs may be any that keep to these rules, and one draw needn't show every extreme that they name: `pair_list`: each row holds a reference date and a strictly later secondary date at most 6 dates after it; no two rows are equal; dates are unevenly used, earlier ones more often.
All inputs are finite; a program needn't handle non-finite values.
Results may differ from a plain program's by a relative error of at most 0.0003.
Values may be sent and summed in bfloat16 or wider, within the bound.
A program may use at most 128 MiB of HBM per device.

v0:
```python
import jax
import jax.numpy as jnp
from jax import lax
from jax.sharding import PartitionSpec as P

PAIR_DEV = 4
ML_ROWS = 5
ML_COLS = 20


def with_halo(block, sides, width):
    for axis, dim in sides:
        count = lax.axis_size(axis)
        forward = [(i, i + 1) for i in range(count - 1)]
        backward = [(target, source) for source, target in forward]
        low = lax.ppermute(
            lax.slice_in_dim(block, block.shape[dim] - width, None, axis=dim), axis, forward
        )
        high = lax.ppermute(lax.slice_in_dim(block, 0, width, axis=dim), axis, backward)
        block = jnp.concatenate([low, block, high], axis=dim)
    return block


def cross_terms(first, second):
    a0 = first[0].astype(jnp.float32)
    a1 = first[1].astype(jnp.float32)
    b0 = second[0].astype(jnp.float32)
    b1 = second[1].astype(jnp.float32)
    return jnp.stack([a0 * b0 + a1 * b1, a1 * b0 - a0 * b1, a0 * a0 + a1 * a1, b0 * b0 + b1 * b1])


def on_device(slc, pair_list, owner):
    pair_dev = PAIR_DEV
    look_rows = slc.shape[2] // ML_ROWS
    slots = lax.dynamic_slice_in_dim(owner, lax.axis_index("wide") * pair_dev, pair_dev)
    chosen = pair_list[slots]
    needed = jnp.concatenate([chosen[:, 0], chosen[:, 1]])
    piece = lax.all_gather(slc, "wide", axis=1, tiled=True)
    count = piece.shape[1]
    onehot = (needed[:, None] == jnp.arange(count, dtype=jnp.int32)[None, :]).astype(jnp.bfloat16)
    picked = jnp.einsum("sp,cprk->csrk", onehot, piece, preferred_element_type=jnp.float32)
    selected = picked.astype(jnp.bfloat16)
    terms = cross_terms(selected[:, :pair_dev], selected[:, pair_dev:])
    band = terms.shape[3]
    looked = terms.reshape(4, pair_dev, look_rows, ML_ROWS, band // ML_COLS, ML_COLS).sum(
        axis=(3, 5)
    )
    padded = with_halo(looked, (("narrow", 2),), 1)
    rowsum = padded[:, :, :-2] + padded[:, :, 1:-1] + padded[:, :, 2:]
    rowsum = jnp.pad(rowsum, ((0, 0), (0, 0), (0, 0), (1, 1)))
    boxed = rowsum[:, :, :, :-2] + rowsum[:, :, :, 1:-1] + rowsum[:, :, :, 2:]
    magnitude = jnp.sqrt(boxed[0] * boxed[0] + boxed[1] * boxed[1])
    coherence = magnitude / jnp.sqrt(boxed[2] * boxed[3] + 1e-06)
    interferogram = looked[:2] / (ML_ROWS * ML_COLS)
    return (interferogram, coherence)


def solution(mesh):
    in_specs = (P(None, ("frames", "wide"), "narrow", None), P(), P())
    out_specs = (P(None, ("frames", "wide"), "narrow", None), P(("frames", "wide"), "narrow", None))
    return jax.shard_map(
        on_device, mesh=mesh, in_specs=in_specs, out_specs=out_specs, check_vma=False
    )
```

profile of v0, /device:TPU:0, one launch (start us, length us, event | category | flops | bytes accessed | tf_op | source)
XLA Modules:
  0.0 177.0 jit_solution(9089996930540128313)
XLA Ops:
  7.2 0.0 all-gather.2.cloned.1.call-start
  7.2 2.9 %copy.18 = bf16[2,2,20,5120]{3,0,2,1:T(2,128)(2,1)} copy(bf16[2,2,20,5120]{3,1,2,0:T(2,128)(2,1)} %param.3) | data formatting | bytes 1638400 | tf_op args[0]
  10.1 0.0 all-gather.2.cloned.1.call-update
  10.1 0.8 copy.17
  10.9 0.7 compare_select_fusion
  11.6 0.6 gather_fusion
  12.2 0.2 slice_reduce_fusion.1
  12.4 0.1 pad_add_fusion
  12.4 66.2 %all-gather.2.cloned.1.call-done = bf16[2,8,20,5120]{3,0,2,1:T(2,128)(2,1)} async-done(((bf16[2,2,20,5120]{3,0,2,1:T(2,128)(2,1)}), bf16[2,8,20,5120]{3,0,2,1:T(2,128)(2,1)}) %all-gather.2.cloned.1.call-update) | async-done | bytes 3276816 | tf_op jit(solution)/shard_map/all_gather | solution.py:38
  78.6 5.6 %fusion = bf16[2,8,20,5120]{3,1,2,0:T(8,128)(2,1)S(1)} fusion(bf16[2,8,20,5120]{3,0,2,1:T(2,128)(2,1)} %all-gather.2.cloned.1.call-done, s32[8]{0:T(128)S(1)} %pad_add_fusion), kind=kOutput, calls=%fused_computation.3 | convolution fusion | flops 27852864 | bytes 6553632 | tf_op jit(solution)/shard_map/sp,cprk->csrk/dot_general | solution.py:41
  84.2 3.5 %fusion.3 = (f32[1,4,20,5120]{3,1,2,0:T(4,128)}, f32[1,4,20,5120]{3,1,2,0:T(4,128)}, f32[1,4,20,5120]{3,1,2,0:T(4,128)S(1)}, f32[1,4,20,5120]{3,1,2,0:T(4,128)S(1)}) fusion(bf16[2,8,20,5120]{3,1,2,0:T(8,128)(2,1)S(1)} %fusion), kind=kLoop, calls=%fused_computation.14 | loop fusion | flops 6553600 | bytes 9830400 | tf_op jit(solution)/shard_map/add | solution.py:29
  87.7 14.8 %stack.15 = f32[1,4,4,5,256,20]{5,4,1,3,2,0:T(8,128)} reshape(f32[1,4,20,5120]{3,1,2,0:T(4,128)} %get-tuple-element.8) | data formatting | bytes 3276800 | tf_op jit(solution)/shard_map/stack | solution.py:29
  102.5 14.7 %stack.17 = f32[1,4,4,5,256,20]{5,4,1,3,2,0:T(8,128)} reshape(f32[1,4,20,5120]{3,1,2,0:T(4,128)} %get-tuple-element.9) | data formatting | bytes 3276800 | tf_op jit(solution)/shard_map/stack | solution.py:29
  117.2 13.7 %stack.18 = f32[1,4,4,5,256,20]{5,4,1,3,2,0:T(8,128)} reshape(f32[1,4,20,5120]{3,1,2,0:T(4,128)S(1)} %get-tuple-element.10) | data formatting | bytes 3276800 | tf_op jit(solution)/shard_map/stack | solution.py:29
  130.9 13.7 %stack.16 = f32[1,4,4,5,256,20]{5,4,1,3,2,0:T(8,128)} reshape(f32[1,4,20,5120]{3,1,2,0:T(4,128)S(1)} %get-tuple-element.11) | data formatting | bytes 3276800 | tf_op jit(solution)/shard_map/stack | solution.py:29
  144.6 18.6 %maximum_reduce_fusion = f32[4,4,4,256]{3,1,2,0:T(4,128)S(1)} fusion(f32[1,4,4,5,256,20]{5,4,1,3,2,0:T(8,128)} %stack.18, f32[1,4,4,5,256,20]{5,4,1,3,2,0:T(8,128)} %stack.17, f32[1,4,4,5,256,20]{5,4,1,3,2,0:T(8,128)} %stack.16, f32[1,4,4,5,256,20]{5,4,1,3,2,0:T(8,128)} %stack.15), kind=kLoop, calls=%fused_computation.1 | loop fusion | flops 6537216 | bytes 6619136 | tf_op jit(solution)/shard_map/reduce_sum | solution.py:45
  163.2 1.7 collective-permute-start
  164.9 1.3 collective-permute-start.1
  166.3 0.6 copy.20
  166.9 0.0 collective-permute-done
  166.9 2.4 %collective-permute-done.1 = f32[4,4,1,256]{3,1,2,0:T(4,128)S(1)} collective-permute-done((f32[4,4,1,256]{3,1,2,0:T(4,128)S(1)}, f32[4,4,1,256]{3,1,2,0:T(4,128)S(1)}, u32[]{:S(2)}, u32[]{:S(2)}) %collective-permute-start.1) | collective-permute-done | bytes 16416 | tf_op jit(solution)/shard_map/ppermute | solution.py:19
  169.3 0.1 fusion.7
  169.5 0.6 copy.21
  (5 shorter events, 0.1 us)
Async XLA Ops:
  7.2 71.5 %all-gather.2.cloned.1.call-start = ((), (), s32[]{:S(2)}) async-start(), calls=%async_computation | async-start | bytes 4096000 | tf_op jit(solution)/shard_map/all_gather | solution.py:38
  163.2 3.7 %collective-permute-start = (f32[4,4,1,256]{3,1,2,0:T(4,128)S(1)}, f32[4,4,1,256]{3,1,2,0:T(4,128)S(1)}, u32[]{:S(2)}, u32[]{:S(2)}) collective-permute-start(f32[4,4,1,256]{3,1,2,0:T(4,128)S(1)} %get-tuple-element.12), channel_id=1, source_target_pairs={{0,1},{1,2},{2,3},{4,5},{5,6},{6,7},{8,9},{9,10},{10,11},{12,13},{... | collective-permute-start | bytes 49160 | tf_op jit(solution)/shard_map/ppermute | solution.py:16
  164.9 4.4 %collective-permute-start.1 = (f32[4,4,1,256]{3,1,2,0:T(4,128)S(1)}, f32[4,4,1,256]{3,1,2,0:T(4,128)S(1)}, u32[]{:S(2)}, u32[]{:S(2)}) collective-permute-start(f32[4,4,1,256]{3,1,2,0:T(4,128)S(1)} %get-tuple-element.13), channel_id=1, source_target_pairs={{1,0},{2,1},{3,2},{5,4},{6,5},{7,6},{9,8},{10,9},{11,10},{13,12},{... | collective-permute-start | bytes 49160 | tf_op jit(solution)/shard_map/ppermute | solution.py:19
Sparse Core Ops, SparseCore 0:
  10.2 68.3 all-gather.1
where the time goes:
time: 179 us; the launch traced here: 177 us
  waiting for transfers between devices  68.7 us (38%)
  local copies, waits for them, and re-layouts  62.5 us (35%)
  other arithmetic  23.1 us (13%)
  between operations  14.1 us (8%)
  matrix products  5.6 us (3%)
  starting transfers between devices  3.03 us (2%)
    all_gather x1, waiting for transfers between devices, on_device(): piece = lax.all_gather(slc, 'wide', axis=1, tiled=True)  66.2 us
    another operation x4, local copies, waits for them, and re-layouts, cross_terms(): jnp.stack([a0 * b0 + a1 * b1, a1 * b0 - a0 * b1, a0 * a0 + a1 * a1, b0 *...  56.8 us
    reduce_sum x1, other arithmetic, on_device(): terms.reshape(4, pair_dev, look_rows, ML_ROWS, band // ML_COLS, ML_COLS)  18.6 us
    dot_general x1, matrix products, on_device(): jnp.einsum('sp,cprk->csrk', onehot, piece, preferred_element_type=jnp.flo...  5.6 us
    unnamed x4, local copies, waits for them, and re-layouts  4.88 us
  transfers between devices with their start and end apart: 3, of which 2 were waited for; matrix products, arithmetic and copies ran while one was open for 2% of the time, Pallas kernels for 0%

commit v1 on v0

--- a/solution.py
+++ b/solution.py
@@ -1,6 +1,10 @@
+import functools
+
 import jax
 import jax.numpy as jnp
 from jax import lax
+from jax.experimental import pallas as pl
+from jax.experimental.pallas import tpu as pltpu
 from jax.sharding import PartitionSpec as P
 
 PAIR_DEV = 4
@@ -29,7 +33,7 @@
     return jnp.stack([a0 * b0 + a1 * b1, a1 * b0 - a0 * b1, a0 * a0 + a1 * a1, b0 * b0 + b1 * b1])
 
 
-def on_device(slc, pair_list, owner):
+def gathered(slc, pair_list, owner):
     pair_dev = PAIR_DEV
     look_rows = slc.shape[2] // ML_ROWS
     slots = lax.dynamic_slice_in_dim(owner, lax.axis_index("wide") * pair_dev, pair_dev)
@@ -55,9 +59,321 @@
     return (interferogram, coherence)
 
 
+LANES = 128
+
+
+def split_terms(value):
+    high = value.astype(jnp.bfloat16)
+    return high, (value - high.astype(jnp.float32)).astype(jnp.bfloat16)
+
+
+def exchange_kernel(
+    wide, narrow, half, widths, pair_ref, owner_ref, slc_ref, inter_ref, coh_ref,
+    pixels, stage, send_a, send_b, recv_a, recv_b, high_a, low_a, high_b, low_b,
+    looks, message, edges, got, got_edges, grown,
+    load_sem, send_sem, recv_sem, back_send, back_recv, edge_send, edge_recv,
+):
+    me = lax.axis_index("wide")
+    row = lax.axis_index("narrow")
+    above = lax.rem(row + narrow - 1, narrow)
+    below = lax.rem(row + 1, narrow)
+    if wide == 4:
+        targets = [lax.rem(me + 2, wide), wide - 1 - me, me + 1 - 2 * lax.rem(me, 2), me]
+    else:
+        targets = [lax.rem(me + k, wide) for k in range(1, wide + 1)]
+    others = targets[:-1]
+    sends, recvs = (send_a, send_b), (recv_a, recv_b)
+    dates = recv_a.shape[0]
+    pairs = owner_ref.shape[0]
+    look_rows = slc_ref.shape[2] // ML_ROWS
+
+    load = pltpu.make_async_copy(slc_ref, pixels, load_sem)
+    load.start()
+    barrier = pltpu.get_barrier_semaphore()
+    for target in others:
+        pl.semaphore_signal(barrier, inc=1, device_id={"wide": target})
+    for target in targets:
+        for side in (above, below):
+            pl.semaphore_signal(barrier, inc=1, device_id={"wide": target, "narrow": side})
+    load.wait()
+
+    def pack(target, part, dst):
+        width = widths[part]
+        offset = sum(widths[:part])
+        for date in range(2):
+            for comp in range(2):
+                for group in range(2):
+                    column = pl.multiple_of(target * (2 * half) + (group * half + offset), LANES)
+                    block = pixels[comp, date, :, pl.ds(column, width)]
+                    for tile in range(width // LANES):
+                        stage[date, comp * 2 + group, tile, 0:20] = block[
+                            :, tile * LANES : (tile + 1) * LANES
+                        ].astype(jnp.float32)
+            for line in range(ML_ROWS):
+                for tile in range(width // LANES):
+                    rows = [
+                        stage[date, i, tile, pl.ds(line, look_rows, stride=ML_ROWS)]
+                        for i in range(4)
+                    ]
+                    dst[date, line, :, tile * LANES : (tile + 1) * LANES] = jnp.concatenate(
+                        rows, axis=0
+                    ).astype(jnp.bfloat16)
+
+    started = []
+    for part in range(2):
+        for k, target in enumerate(others):
+            pack(target, part, sends[part].at[k])
+            if part == 0 and k == 0:
+                pl.semaphore_wait(barrier, 3 * wide - 1)
+            copy = pltpu.make_async_remote_copy(
+                src_ref=sends[part].at[k],
+                dst_ref=recvs[part].at[pl.ds(2 * me, 2)],
+                send_sem=send_sem.at[part, k],
+                recv_sem=recv_sem.at[part, me],
+                device_id={"wide": target},
+            )
+            copy.start()
+            started.append(copy)
+    for part in range(2):
+        pack(me, part, recvs[part].at[pl.ds(2 * me, 2)])
+
+    looks_half = half // ML_COLS
+
+    def work(part):
+        width = widths[part]
+        offset = sum(widths[:part])
+        recv = recvs[part]
+        high, low = ((high_a, low_a), (high_b, low_b))[part]
+        pixel = lax.broadcasted_iota(jnp.int32, (width, LANES), 0) + offset
+        look = lax.broadcasted_iota(jnp.int32, (width, LANES), 1) & (looks_half - 1)
+        first = look * ML_COLS
+        summer = ((pixel >= first) & (pixel < first + ML_COLS)).astype(jnp.bfloat16)
+
+        for k, target in enumerate(others):
+            pltpu.make_async_remote_copy(
+                src_ref=sends[part].at[k],
+                dst_ref=recv.at[pl.ds(2 * target, 2)],
+                send_sem=send_sem.at[part, k],
+                recv_sem=recv_sem.at[part, target],
+                device_id={"wide": target},
+            ).wait_recv()
+
+        def power(i, carry):
+            both = []
+            for date in range(2):
+                total = jnp.zeros((8, width), jnp.float32)
+                for line in range(ML_ROWS):
+                    value = recv[2 * i + date, line].astype(jnp.float32)
+                    total += value[:8] * value[:8] + value[8:] * value[8:]
+                both.append(total)
+            high[pairs + i], low[pairs + i] = split_terms(jnp.concatenate(both, axis=0))
+            return carry
+
+        lax.fori_loop(0, dates // 2, power, 0)
+
+        def cross(slot, carry):
+            chosen = owner_ref[slot]
+            one, two = pair_ref[chosen, 0], pair_ref[chosen, 1]
+            real = jnp.zeros((8, width), jnp.float32)
+            imag = jnp.zeros((8, width), jnp.float32)
+            for line in range(ML_ROWS):
+                a = recv[one, line].astype(jnp.float32)
+                b = recv[two, line].astype(jnp.float32)
+                real += a[:8] * b[:8] + a[8:] * b[8:]
+                imag += a[8:] * b[:8] - a[:8] * b[8:]
+            high[slot], low[slot] = split_terms(jnp.concatenate([real, imag], axis=0))
+            return carry
+
+        lax.fori_loop(0, pairs, cross, 0)
+        count = high.shape[0] * 16
+        summed = jnp.dot(
+            high[...].reshape(count, width), summer, preferred_element_type=jnp.float32
+        ) + jnp.dot(low[...].reshape(count, width), summer, preferred_element_type=jnp.float32)
+        summed = summed.reshape(count // 8, 8, LANES)
+        if part == 0:
+            looks[...] = summed
+        else:
+            looks[...] += summed
+
+    work(0)
+    work(1)
+
+    sub = lax.broadcasted_iota(jnp.int32, (8, LANES), 0)
+    lane = lax.broadcasted_iota(jnp.int32, (8, LANES), 1)
+    low_half = sub < 4
+    left = lane < 64
+    group_zero = (lane & 32) == 0
+    back = []
+    for k, target in enumerate(targets):
+        own = k == wide - 1
+        for term in range(4):
+            held = jnp.zeros((8, LANES), jnp.float32)
+            for slot in range(PAIR_DEV):
+                place = target * PAIR_DEV + slot
+                if term < 2:
+                    value = looks[2 * place + term]
+                else:
+                    value = looks[2 * pairs + pair_ref[owner_ref[place], term - 2]]
+                turned = pltpu.roll(value, 4, 0)
+                if slot < 2:
+                    value = jnp.where(group_zero, value, turned)
+                else:
+                    value = jnp.where(group_zero, turned, value)
+                here = (low_half if slot < 2 else ~low_half) & (left if slot % 2 == 0 else ~left)
+                held = jnp.where(here, value, held)
+            message[k, 8 * term : 8 * term + 8] = held
+        for side in range(2):
+            edges[k, side] = message[k, pl.ds(3 * side, 8, stride=4)]
+        if own:
+            got[me] = message[k]
+        else:
+            copy = pltpu.make_async_remote_copy(
+                src_ref=message.at[k],
+                dst_ref=got.at[me],
+                send_sem=back_send.at[k],
+                recv_sem=back_recv.at[me],
+                device_id={"wide": target},
+            )
+            copy.start()
+            back.append(copy)
+        for side in range(2):
+            copy = pltpu.make_async_remote_copy(
+                src_ref=edges.at[k, side],
+                dst_ref=got_edges.at[side, me],
+                send_sem=edge_send.at[side, k],
+                recv_sem=edge_recv.at[side, me],
+                device_id={"wide": target, "narrow": (above, below)[side]},
+            )
+            copy.start()
+            back.append(copy)
+
+    for copy in started:
+        copy.wait_send()
+    for k, target in enumerate(targets):
+        if k < wide - 1:
+            pltpu.make_async_remote_copy(
+                src_ref=message.at[k],
+                dst_ref=got.at[target],
+                send_sem=back_send.at[k],
+                recv_sem=back_recv.at[target],
+                device_id={"wide": target},
+            ).wait_recv()
+        for side in range(2):
+            pltpu.make_async_remote_copy(
+                src_ref=edges.at[k, side],
+                dst_ref=got_edges.at[side, target],
+                send_sem=edge_send.at[side, k],
+                recv_sem=edge_recv.at[side, target],
+                device_id={"wide": target, "narrow": (above, below)[side]},
+            ).wait_recv()
+
+    def across(parts, parity):
+        tiles = []
+        for i in range(0, wide, 2):
+            one, two = parts[i], parts[i + 1]
+            if parity == 0:
+                tiles.append(jnp.where(left, one, pltpu.roll(two, 64, 1)))
+            else:
+                tiles.append(jnp.where(left, pltpu.roll(one, 64, 1), two))
+        return jnp.concatenate(tiles, axis=1)
+
+    for parity in range(2):
+        top = across([got_edges[1, w] for w in range(wide)], parity)
+        bottom = across([got_edges[0, w] for w in range(wide)], parity)
+        top = jnp.where(row == 0, 0.0, top)
+        bottom = jnp.where(row == narrow - 1, 0.0, bottom)
+        for term in range(4):
+            middle = across([got[w, 8 * term : 8 * term + 8] for w in range(wide)], parity)
+            for upper in range(2):
+                slot = 2 * upper + parity
+                edge = 2 * term + upper
+                grown[term, slot, 0:1] = top[edge : edge + 1]
+                grown[term, slot, 1:5] = middle[4 * upper : 4 * upper + 4]
+                grown[term, slot, 5:6] = bottom[edge : edge + 1]
+
+    columns = wide * 64
+    place = lax.broadcasted_iota(jnp.int32, (4, columns), 1)
+    for slot in range(PAIR_DEV):
+        boxed = []
+        for term in range(4):
+            rows = grown[term, slot, 0:4] + grown[term, slot, 1:5] + grown[term, slot, 2:6]
+            before = jnp.where(place == 0, 0.0, pltpu.roll(rows, 1, 1))
+            after = jnp.where(place == columns - 1, 0.0, pltpu.roll(rows, columns - 1, 1))
+            boxed.append(before + rows + after)
+            if term < 2:
+                inter_ref[term, slot] = grown[term, slot, 1:5] / (ML_ROWS * ML_COLS)
+        magnitude = jnp.sqrt(boxed[0] * boxed[0] + boxed[1] * boxed[1])
+        coh_ref[slot] = magnitude / jnp.sqrt(boxed[2] * boxed[3] + 1e-06)
+
+    for copy in back:
+        copy.wait_send()
+
+
+def exchanged(slc, pair_list, owner):
+    wide = lax.axis_size("wide")
+    narrow = lax.axis_size("narrow")
+    columns = slc.shape[3]
+    half = columns // wide // 2
+    first = half // 2 // LANES * LANES
+    widths = (first, half - first)
+    pairs = owner.shape[0]
+    dates = 2 * wide
+    blocks = pairs + dates // 2
+    bf16, f32 = jnp.bfloat16, jnp.float32
+    scratch = [
+        pltpu.VMEM(slc.shape, bf16),
+        pltpu.VMEM((2, 4, widths[1] // LANES, 24, LANES), f32),
+    ]
+    scratch += [pltpu.VMEM((wide - 1, 2, ML_ROWS, 16, n), bf16) for n in widths]
+    scratch += [pltpu.VMEM((dates, ML_ROWS, 16, n), bf16) for n in widths]
+    scratch += [pltpu.VMEM((blocks, 16, n), bf16) for n in widths for _ in range(2)]
+    scratch += [
+        pltpu.VMEM((2 * blocks, 8, LANES), f32),
+        pltpu.VMEM((wide, 32, LANES), f32),
+        pltpu.VMEM((wide, 2, 8, LANES), f32),
+        pltpu.VMEM((wide, 32, LANES), f32),
+        pltpu.VMEM((2, wide, 8, LANES), f32),
+        pltpu.VMEM((4, PAIR_DEV, 8, wide * 64), f32),
+        pltpu.SemaphoreType.DMA,
+        pltpu.SemaphoreType.DMA((2, wide - 1)),
+        pltpu.SemaphoreType.DMA((2, wide)),
+        pltpu.SemaphoreType.DMA((wide,)),
+        pltpu.SemaphoreType.DMA((wide,)),
+        pltpu.SemaphoreType.DMA((2, wide)),
+        pltpu.SemaphoreType.DMA((2, wide)),
+    ]
+    look_rows = slc.shape[2] // ML_ROWS
+    look_columns = columns // ML_COLS
+    return pl.pallas_call(
+        functools.partial(exchange_kernel, wide, narrow, half, widths),
+        out_shape=(
+            jax.ShapeDtypeStruct((2, PAIR_DEV, look_rows, look_columns), f32),
+            jax.ShapeDtypeStruct((PAIR_DEV, look_rows, look_columns), f32),
+        ),
+        in_specs=[
+            pl.BlockSpec(memory_space=pltpu.SMEM),
+            pl.BlockSpec(memory_space=pltpu.SMEM),
+            pl.BlockSpec(memory_space=pl.ANY),
+        ],
+        out_specs=(pl.BlockSpec(memory_space=pltpu.VMEM), pl.BlockSpec(memory_space=pltpu.VMEM)),
+        scratch_shapes=scratch,
+        compiler_params=pltpu.CompilerParams(
+            collective_id=0, has_side_effects=True, vmem_limit_bytes=32 * 1024 * 1024
+        ),
+    )(pair_list, owner, slc)
+
+
 def solution(mesh):
     in_specs = (P(None, ("frames", "wide"), "narrow", None), P(), P())
     out_specs = (P(None, ("frames", "wide"), "narrow", None), P(("frames", "wide"), "narrow", None))
+
+    def on_device(slc, pair_list, owner):
+        wide, narrow = mesh.shape["wide"], mesh.shape["narrow"]
+        tiled = slc.shape[3] == wide * 2 * ML_COLS * 32
+        if tiled and narrow > 2 and wide % 2 == 0 and slc.shape[1:3] == (2, 4 * ML_ROWS):
+            return exchanged(slc, pair_list, owner)
+        return gathered(slc, pair_list, owner)
+
     return jax.shard_map(
         on_device, mesh=mesh, in_specs=in_specs, out_specs=out_specs, check_vma=False
     )

time: 179 us -> 35.2 us (0.20); the launches traced: 177 us -> 35.1 us
  waiting for transfers between devices: 68.7 us -> 0 us
  local copies, waits for them, and re-layouts: 62.5 us -> 3.3 us
  Pallas kernels: 0 us -> 31.1 us
  other arithmetic: 23.1 us -> 0 us
  between operations: 14.1 us -> 0.65 us
  matrix products: 5.6 us -> 0 us
  starting transfers between devices: 3.03 us -> 0 us
    all_gather x1 -> x0, waiting for transfers between devices: 66.2 us -> none  [on_device(): piece = lax.all_gather(slc, 'wide', axis=1, tiled=True)]
    another operation x4 -> x0, local copies, waits for them, and re-layouts: 56.8 us -> none  [cross_terms(): jnp.stack([a0 * b0 + a1 * b1, a1 * b0 - a0 * b1, a0 * a0 + a1 * a1, b0 *...]
    pallas_call x0 -> x1, Pallas kernels: none -> 31.1 us  [exchanged(): pl.pallas_call(functools.partial(exchange_kernel, wide, narrow, half, wid...]
    reduce_sum x1 -> x0, other arithmetic: 18.6 us -> none  [on_device(): terms.reshape(4, pair_dev, look_rows, ML_ROWS, band // ML_COLS, ML_COLS)]
    dot_general x1 -> x0, matrix products: 5.6 us -> none  [on_device(): jnp.einsum('sp,cprk->csrk', onehot, piece, preferred_element_type=jnp.flo...]
    add x3 -> x0, other arithmetic: 3.65 us -> none  [the longest x1 3.5 us: cross_terms(): a0 * b0 + a1 * b1]
    ppermute x2 -> x0, starting transfers between devices: 2.99 us -> none  [the longest x1 1.7 us: with_halo(): lax.ppermute(lax.slice_in_dim(block, block.shape[dim] - width, None, axis...]
    ppermute x2 -> x0, waiting for transfers between devices: 2.43 us -> none  [the longest x1 2.43 us: with_halo(): lax.ppermute(lax.slice_in_dim(block, 0, width, axis=dim), axis, backward)]
  transfers between devices with their start and end apart: 3 -> 0, of which waited for: 2 -> 0; matrix products, arithmetic and copies ran while one was open for 2% -> 0% of each run, Pallas kernels for 0% -> 0%
where the time goes in v1:
time: 35.2 us; the launch traced here: 35.1 us
  Pallas kernels  31.1 us (88%)
  local copies, waits for them, and re-layouts  3.3 us (9%)
  between operations  0.65 us (2%)
    pallas_call x1, Pallas kernels, exchanged(): pl.pallas_call(functools.partial(exchange_kernel, wide, narrow, half, wid...  31.1 us
    unnamed x6, local copies, waits for them, and re-layouts  3.3 us

profile of v1, /device:TPU:0, one launch (start us, length us, event | category | flops | bytes accessed | tf_op | source)
XLA Modules:
  0.0 35.1 jit_solution(283167780944667091)
XLA Ops:
  0.6 0.8 %copy.5.pair_ref = s32[16,2]{1,0:T(8,128)S(1)} copy(s32[16,2]{0,1:T(2,128)} %param.4) | data formatting | bytes 256 | tf_op args[1]
  1.4 0.0 copy-start
  1.4 1.3 %copy.6.slc_ref = bf16[2,2,20,5120]{3,2,1,0:T(8,128)(2,1)S(1)} copy(bf16[2,2,20,5120]{3,1,2,0:T(2,128)(2,1)} %param.3) | data formatting | bytes 1638400 | tf_op args[0]
  2.7 0.0 copy-done
  2.7 31.1 %shard_map.50 = (f32[2,4,4,256]{3,2,1,0:T(4,128)S(1)}, f32[4,4,256]{2,1,0:T(4,128)S(1)}) custom-call(s32[16,2]{1,0:T(8,128)S(1)} %copy.5.pair_ref, s32[16]{0:T(128)S(1)} %copy-done, bf16[2,2,20,5120]{3,2,1,0:T(8,128)(2,1)S(1)} %copy.6.slc_ref), custom_call_target="tpu_custom_call" | custom-call | tf_op jit(solution)/shard_map/pallas_call | solution.py:347
  33.8 0.6 %copy.9 = f32[2,4,4,256]{3,2,1,0:T(4,128)} copy(f32[2,4,4,256]{3,2,1,0:T(4,128)S(1)} %get-tuple-element.4) | data formatting | bytes 65536
  34.5 0.6 %copy.10 = f32[4,4,256]{2,1,0:T(4,128)} copy(f32[4,4,256]{2,1,0:T(4,128)S(1)} %get-tuple-element.5) | data formatting | bytes 32768
Async XLA Ops:
  1.4 1.3 %copy-start = (s32[16]{0:T(128)S(1)}, s32[16]{0:T(128)}, u32[]{:S(2)}) copy-start(s32[16]{0:T(128)} %owner_ref.1) | copy-start | bytes 196

commit v2 on v1

--- a/solution.py
+++ b/solution.py
@@ -60,6 +60,8 @@
 
 
 LANES = 128
+PART = 256
+WINDOW = 9
 
 
 def split_terms(value):
@@ -68,9 +70,8 @@
 
 
 def exchange_kernel(
-    wide, narrow, half, widths, pair_ref, owner_ref, slc_ref, inter_ref, coh_ref,
-    pixels, stage, send_a, send_b, recv_a, recv_b, high_a, low_a, high_b, low_b,
-    looks, message, edges, got, got_edges, grown,
+    wide, narrow, half, widths, window, pair_ref, owner_ref, slc_ref, inter_ref, coh_ref,
+    pixels, stage, sends, recvs, highs, lows, looks, message, edges, got, got_edges, grown,
     load_sem, send_sem, recv_sem, back_send, back_recv, edge_send, edge_recv,
 ):
     me = lax.axis_index("wide")
@@ -82,37 +83,44 @@
     else:
         targets = [lax.rem(me + k, wide) for k in range(1, wide + 1)]
     others = targets[:-1]
-    sends, recvs = (send_a, send_b), (recv_a, recv_b)
-    dates = recv_a.shape[0]
+    dates = recvs[0].shape[0]
+    parts = len(widths)
     pairs = owner_ref.shape[0]
-    look_rows = slc_ref.shape[2] // ML_ROWS
-
-    load = pltpu.make_async_copy(slc_ref, pixels, load_sem)
-    load.start()
+    lines = slc_ref.shape[1]
+    look_rows = lines // ML_ROWS
+
+    loads = []
+    for k, target in enumerate(targets):
+        band = pl.ds(pl.multiple_of(target * (2 * half), LANES), 2 * half)
+        load = pltpu.make_async_copy(
+            slc_ref.at[:, :, :, band], pixels.at[:, :, :, band], load_sem.at[k]
+        )
+        load.start()
+        loads.append(load)
     barrier = pltpu.get_barrier_semaphore()
     for target in others:
         pl.semaphore_signal(barrier, inc=1, device_id={"wide": target})
     for target in targets:
         for side in (above, below):
             pl.semaphore_signal(barrier, inc=1, device_id={"wide": target, "narrow": side})
-    load.wait()
 
     def pack(target, part, dst):
         width = widths[part]
         offset = sum(widths[:part])
+        for comp in range(2):
+            for group in range(2):
+                column = pl.multiple_of(target * (2 * half) + (group * half + offset), LANES)
+                for line in range(lines):
+                    block = pixels[comp, line, :, pl.ds(column, width)].astype(jnp.float32)
+                    for tile in range(width // LANES):
+                        stage[comp * 2 + group, tile, 2 * line : 2 * line + 2] = block[
+                            :, tile * LANES : (tile + 1) * LANES
+                        ]
         for date in range(2):
-            for comp in range(2):
-                for group in range(2):
-                    column = pl.multiple_of(target * (2 * half) + (group * half + offset), LANES)
-                    block = pixels[comp, date, :, pl.ds(column, width)]
-                    for tile in range(width // LANES):
-                        stage[date, comp * 2 + group, tile, 0:20] = block[
-                            :, tile * LANES : (tile + 1) * LANES
-                        ].astype(jnp.float32)
             for line in range(ML_ROWS):
                 for tile in range(width // LANES):
                     rows = [
-                        stage[date, i, tile, pl.ds(line, look_rows, stride=ML_ROWS)]
+                        stage[i, tile, pl.ds(2 * line + date, look_rows, stride=2 * ML_ROWS)]
                         for i in range(4)
                     ]
                     dst[date, line, :, tile * LANES : (tile + 1) * LANES] = jnp.concatenate(
@@ -120,8 +128,11 @@
                     ).astype(jnp.bfloat16)
 
     started = []
-    for part in range(2):
+
+    def send(part):
         for k, target in enumerate(others):
+            if part == 0:
+                loads[k].wait()
             pack(target, part, sends[part].at[k])
             if part == 0 and k == 0:
                 pl.semaphore_wait(barrier, 3 * wide - 1)
@@ -134,7 +145,11 @@
             )
             copy.start()
             started.append(copy)
-    for part in range(2):
+
+    for part in range(min(window, parts)):
+        send(part)
+    loads[-1].wait()
+    for part in range(parts):
         pack(me, part, recvs[part].at[pl.ds(2 * me, 2)])
 
     looks_half = half // ML_COLS
@@ -143,7 +158,7 @@
         width = widths[part]
         offset = sum(widths[:part])
         recv = recvs[part]
-        high, low = ((high_a, low_a), (high_b, low_b))[part]
+        high, low = highs[part], lows[part]
         pixel = lax.broadcasted_iota(jnp.int32, (width, LANES), 0) + offset
         look = lax.broadcasted_iota(jnp.int32, (width, LANES), 1) & (looks_half - 1)
         first = look * ML_COLS
@@ -169,11 +184,11 @@
             high[pairs + i], low[pairs + i] = split_terms(jnp.concatenate(both, axis=0))
             return carry
 
-        lax.fori_loop(0, dates // 2, power, 0)
+        lax.fori_loop(0, dates // 2, power, 0, unroll=2)
 
         def cross(slot, carry):
             chosen = owner_ref[slot]
-            one, two = pair_ref[chosen, 0], pair_ref[chosen, 1]
+            one, two = pair_ref[0, chosen], pair_ref[1, chosen]
             real = jnp.zeros((8, width), jnp.float32)
             imag = jnp.zeros((8, width), jnp.float32)
             for line in range(ML_ROWS):
@@ -184,7 +199,7 @@
             high[slot], low[slot] = split_terms(jnp.concatenate([real, imag], axis=0))
             return carry
 
-        lax.fori_loop(0, pairs, cross, 0)
+        lax.fori_loop(0, pairs, cross, 0, unroll=4)
         count = high.shape[0] * 16
         summed = jnp.dot(
             high[...].reshape(count, width), summer, preferred_element_type=jnp.float32
@@ -195,8 +210,12 @@
         else:
             looks[...] += summed
 
-    work(0)
-    work(1)
+    for part in range(parts):
+        if part + window < parts:
+            for copy in started[part * len(others) : (part + 1) * len(others)]:
+                copy.wait_send()
+            send(part + window)
+        work(part)
 
     sub = lax.broadcasted_iota(jnp.int32, (8, LANES), 0)
     lane = lax.broadcasted_iota(jnp.int32, (8, LANES), 1)
@@ -213,7 +232,7 @@
                 if term < 2:
                     value = looks[2 * place + term]
                 else:
-                    value = looks[2 * pairs + pair_ref[owner_ref[place], term - 2]]
+                    value = looks[2 * pairs + pair_ref[term - 2, owner_ref[place]]]
                 turned = pltpu.roll(value, 4, 0)
                 if slot < 2:
                     value = jnp.where(group_zero, value, turned)
@@ -247,7 +266,7 @@
             copy.start()
             back.append(copy)
 
-    for copy in started:
+    for copy in started[max(parts - window, 0) * len(others) :]:
         copy.wait_send()
     for k, target in enumerate(targets):
         if k < wide - 1:
@@ -314,19 +333,21 @@
     narrow = lax.axis_size("narrow")
     columns = slc.shape[3]
     half = columns // wide // 2
-    first = half // 2 // LANES * LANES
-    widths = (first, half - first)
+    widths = tuple(min(PART, half - i) for i in range(0, half, PART))
     pairs = owner.shape[0]
     dates = 2 * wide
     blocks = pairs + dates // 2
     bf16, f32 = jnp.bfloat16, jnp.float32
     scratch = [
-        pltpu.VMEM(slc.shape, bf16),
-        pltpu.VMEM((2, 4, widths[1] // LANES, 24, LANES), f32),
+        pltpu.VMEM((2, slc.shape[2], 2, columns), bf16),
+        pltpu.VMEM((4, widths[0] // LANES, 2 * slc.shape[2], LANES), f32),
     ]
-    scratch += [pltpu.VMEM((wide - 1, 2, ML_ROWS, 16, n), bf16) for n in widths]
-    scratch += [pltpu.VMEM((dates, ML_ROWS, 16, n), bf16) for n in widths]
-    scratch += [pltpu.VMEM((blocks, 16, n), bf16) for n in widths for _ in range(2)]
+    scratch += [
+        [pltpu.VMEM((wide - 1, 2, ML_ROWS, 16, n), bf16) for n in widths],
+        [pltpu.VMEM((dates, ML_ROWS, 16, n), bf16) for n in widths],
+        [pltpu.VMEM((blocks, 16, n), bf16) for n in widths],
+        [pltpu.VMEM((blocks, 16, n), bf16) for n in widths],
+    ]
     scratch += [
         pltpu.VMEM((2 * blocks, 8, LANES), f32),
         pltpu.VMEM((wide, 32, LANES), f32),
@@ -334,9 +355,9 @@
         pltpu.VMEM((wide, 32, LANES), f32),
         pltpu.VMEM((2, wide, 8, LANES), f32),
         pltpu.VMEM((4, PAIR_DEV, 8, wide * 64), f32),
-        pltpu.SemaphoreType.DMA,
-        pltpu.SemaphoreType.DMA((2, wide - 1)),
-        pltpu.SemaphoreType.DMA((2, wide)),
+        pltpu.SemaphoreType.DMA((wide,)),
+        pltpu.SemaphoreType.DMA((len(widths), wide - 1)),
+        pltpu.SemaphoreType.DMA((len(widths), wide)),
         pltpu.SemaphoreType.DMA((wide,)),
         pltpu.SemaphoreType.DMA((wide,)),
         pltpu.SemaphoreType.DMA((2, wide)),
@@ -345,22 +366,22 @@
     look_rows = slc.shape[2] // ML_ROWS
     look_columns = columns // ML_COLS
     return pl.pallas_call(
-        functools.partial(exchange_kernel, wide, narrow, half, widths),
+        functools.partial(exchange_kernel, wide, narrow, half, widths, WINDOW),
         out_shape=(
-            jax.ShapeDtypeStruct((2, PAIR_DEV, look_rows, look_columns), f32),
-            jax.ShapeDtypeStruct((PAIR_DEV, look_rows, look_columns), f32),
+            pltpu.VMEM((2, PAIR_DEV, look_rows, look_columns), f32),
+            pltpu.VMEM((PAIR_DEV, look_rows, look_columns), f32),
         ),
         in_specs=[
             pl.BlockSpec(memory_space=pltpu.SMEM),
             pl.BlockSpec(memory_space=pltpu.SMEM),
-            pl.BlockSpec(memory_space=pl.ANY),
+            pl.BlockSpec(memory_space=pltpu.HBM),
         ],
         out_specs=(pl.BlockSpec(memory_space=pltpu.VMEM), pl.BlockSpec(memory_space=pltpu.VMEM)),
         scratch_shapes=scratch,
         compiler_params=pltpu.CompilerParams(
-            collective_id=0, has_side_effects=True, vmem_limit_bytes=32 * 1024 * 1024
+            collective_id=0, has_side_effects=True, vmem_limit_bytes=56 * 1024 * 1024
         ),
-    )(pair_list, owner, slc)
+    )(*(pltpu.with_memory_space_constraint(x, pltpu.HBM) for x in (pair_list.T, owner, slc.transpose(0, 2, 1, 3))))
 
 
 def solution(mesh):

time: 35.2 us -> 33 us (0.937)
  local copies, waits for them, and re-layouts: 3.3 us -> 1.22 us
    unnamed x6 -> x2, local copies, waits for them, and re-layouts: 3.3 us -> 1.22 us
where the time goes in v2:
time: 33 us; the launch traced here: 32.8 us
  Pallas kernels  31 us (94%)
  local copies, waits for them, and re-layouts  1.22 us (4%)
  between operations  0.64 us (2%)
    pallas_call x1, Pallas kernels, exchanged(): pl.pallas_call(functools.partial(exchange_kernel, wide, narrow, half, wid...  31 us
    unnamed x2, local copies, waits for them, and re-layouts  1.22 us

profile of v2, /device:TPU:0, one launch (start us, length us, event | category | flops | bytes accessed | tf_op | source)
XLA Modules:
  0.0 32.8 jit_solution(10271037231058588898)
XLA Ops:
  0.6 31.0 %shard_map.50 = (f32[2,4,4,256]{3,2,1,0:T(4,128)S(1)}, f32[4,4,256]{2,1,0:T(4,128)S(1)}) custom-call(s32[2,16]{1,0:T(2,128)} %bitcast.3, s32[16]{0:T(128)} %owner_ref.1, bf16[2,20,2,5120]{3,2,1,0:T(2,128)(2,1)} %bitcast.2), custom_call_target="tpu_custom_call" | custom-call | tf_op jit(solution)/shard_map/pallas_call | solution.py:368
  31.6 0.6 %copy.7 = f32[2,4,4,256]{3,2,1,0:T(4,128)} copy(f32[2,4,4,256]{3,2,1,0:T(4,128)S(1)} %get-tuple-element.2) | data formatting | bytes 65536
  32.2 0.6 %copy.8 = f32[4,4,256]{2,1,0:T(4,128)} copy(f32[4,4,256]{2,1,0:T(4,128)S(1)} %get-tuple-element.3) | data formatting | bytes 32768

commit v3 on v2

--- a/solution.py
+++ b/solution.py
@@ -61,7 +61,6 @@
 
 LANES = 128
 PART = 256
-WINDOW = 9
 
 
 def split_terms(value):
@@ -70,20 +69,18 @@
 
 
 def exchange_kernel(
-    wide, narrow, half, widths, window, pair_ref, owner_ref, slc_ref, inter_ref, coh_ref,
-    pixels, stage, sends, recvs, highs, lows, looks, message, edges, got, got_edges, grown,
+    wide, narrow, half, widths, pair_ref, owner_ref, slc_ref, inter_ref, coh_ref,
+    pixels, stage, sends, recvs, highs, lows, looks, message, edges, got, got_edges,
+    own_power, own_rims, power, rims, grown, below_line,
     load_sem, send_sem, recv_sem, back_send, back_recv, edge_send, edge_recv,
+    power_send, power_recv, rim_send, rim_recv,
 ):
     me = lax.axis_index("wide")
     row = lax.axis_index("narrow")
     above = lax.rem(row + narrow - 1, narrow)
     below = lax.rem(row + 1, narrow)
-    if wide == 4:
-        targets = [lax.rem(me + 2, wide), wide - 1 - me, me + 1 - 2 * lax.rem(me, 2), me]
-    else:
-        targets = [lax.rem(me + k, wide) for k in range(1, wide + 1)]
+    targets = [lax.rem(me + 2, wide), wide - 1 - me, me + 1 - 2 * lax.rem(me, 2), me]
     others = targets[:-1]
-    dates = recvs[0].shape[0]
     parts = len(widths)
     pairs = owner_ref.shape[0]
     lines = slc_ref.shape[1]
@@ -146,7 +143,7 @@
             copy.start()
             started.append(copy)
 
-    for part in range(min(window, parts)):
+    for part in range(parts):
         send(part)
     loads[-1].wait()
     for part in range(parts):
@@ -154,16 +151,55 @@
 
     looks_half = half // ML_COLS
 
-    def work(part):
+    def summer(part):
         width = widths[part]
         offset = sum(widths[:part])
-        recv = recvs[part]
-        high, low = highs[part], lows[part]
         pixel = lax.broadcasted_iota(jnp.int32, (width, LANES), 0) + offset
         look = lax.broadcasted_iota(jnp.int32, (width, LANES), 1) & (looks_half - 1)
         first = look * ML_COLS
-        summer = ((pixel >= first) & (pixel < first + ML_COLS)).astype(jnp.bfloat16)
-
+        return ((pixel >= first) & (pixel < first + ML_COLS)).astype(jnp.bfloat16)
+
+    def add_looks(part, begin, end):
+        width = widths[part]
+        count = (end - begin) * 16
+        spread = summer(part)
+        summed = jnp.dot(
+            highs[part][begin:end].reshape(count, width),
+            spread,
+            preferred_element_type=jnp.float32,
+        ) + jnp.dot(
+            lows[part][begin:end].reshape(count, width),
+            spread,
+            preferred_element_type=jnp.float32,
+        )
+        summed = summed.reshape(count // 8, 8, LANES)
+        if part == 0:
+            looks[2 * begin : 2 * end] = summed
+        else:
+            looks[2 * begin : 2 * end] += summed
+
+    def powers(part):
+        width = widths[part]
+        for k in range(wide):
+            both = []
+            for date in range(2):
+                total = jnp.zeros((8, width), jnp.float32)
+                for line in range(ML_ROWS):
+                    if k < wide - 1:
+                        value = sends[part][k, date, line].astype(jnp.float32)
+                    else:
+                        value = recvs[part][2 * me + date, line].astype(jnp.float32)
+                    total += value[:8] * value[:8] + value[8:] * value[8:]
+                both.append(total)
+            highs[part][pairs + k], lows[part][pairs + k] = split_terms(
+                jnp.concatenate(both, axis=0)
+            )
+        add_looks(part, pairs, pairs + wide)
+
+    def work(part):
+        width = widths[part]
+        recv = recvs[part]
+        high, low = highs[part], lows[part]
         for k, target in enumerate(others):
             pltpu.make_async_remote_copy(
                 src_ref=sends[part].at[k],
@@ -172,19 +208,6 @@
                 recv_sem=recv_sem.at[part, target],
                 device_id={"wide": target},
             ).wait_recv()
-
-        def power(i, carry):
-            both = []
-            for date in range(2):
-                total = jnp.zeros((8, width), jnp.float32)
-                for line in range(ML_ROWS):
-                    value = recv[2 * i + date, line].astype(jnp.float32)
-                    total += value[:8] * value[:8] + value[8:] * value[8:]
-                both.append(total)
-            high[pairs + i], low[pairs + i] = split_terms(jnp.concatenate(both, axis=0))
-            return carry
-
-        lax.fori_loop(0, dates // 2, power, 0, unroll=2)
 
         def cross(slot, carry):
             chosen = owner_ref[slot]
@@ -200,39 +223,64 @@
             return carry
 
         lax.fori_loop(0, pairs, cross, 0, unroll=4)
-        count = high.shape[0] * 16
-        summed = jnp.dot(
-            high[...].reshape(count, width), summer, preferred_element_type=jnp.float32
-        ) + jnp.dot(low[...].reshape(count, width), summer, preferred_element_type=jnp.float32)
-        summed = summed.reshape(count // 8, 8, LANES)
-        if part == 0:
-            looks[...] = summed
-        else:
-            looks[...] += summed
-
-    for part in range(parts):
-        if part + window < parts:
-            for copy in started[part * len(others) : (part + 1) * len(others)]:
-                copy.wait_send()
-            send(part + window)
-        work(part)
+        add_looks(part, 0, pairs)
 
     sub = lax.broadcasted_iota(jnp.int32, (8, LANES), 0)
     lane = lax.broadcasted_iota(jnp.int32, (8, LANES), 1)
     low_half = sub < 4
     left = lane < 64
     group_zero = (lane & 32) == 0
+
+    for part in range(parts):
+        powers(part)
+    for date in range(2):
+        held = jnp.zeros((8, LANES), jnp.float32)
+        for k, target in enumerate(targets):
+            held = jnp.where(lane // looks_half == target, looks[2 * (pairs + k) + date], held)
+        own_power[date] = held
+        for side in range(2):
+            own_rims[side, date] = own_power[date, pl.ds(3 * side, 2, stride=4)]
+    power[pl.ds(2 * me, 2)] = own_power[...]
+
     back = []
+
+    def send_powers():
+        for k, target in enumerate(targets):
+            if k < wide - 1:
+                copy = pltpu.make_async_remote_copy(
+                    src_ref=own_power,
+                    dst_ref=power.at[pl.ds(2 * me, 2)],
+                    send_sem=power_send.at[k],
+                    recv_sem=power_recv.at[me],
+                    device_id={"wide": target},
+                )
+                copy.start()
+                back.append(copy)
+            for side in range(2):
+                copy = pltpu.make_async_remote_copy(
+                    src_ref=own_rims.at[side],
+                    dst_ref=rims.at[side, pl.ds(2 * me, 2)],
+                    send_sem=rim_send.at[side, k],
+                    recv_sem=rim_recv.at[side, me],
+                    device_id={"wide": target, "narrow": (above, below)[side]},
+                )
+                copy.start()
+                back.append(copy)
+
+    for part in range(parts):
+        if part == parts - 1:
+            for copy in started:
+                copy.wait_send()
+            send_powers()
+        work(part)
+
     for k, target in enumerate(targets):
         own = k == wide - 1
-        for term in range(4):
+        for term in range(2):
             held = jnp.zeros((8, LANES), jnp.float32)
             for slot in range(PAIR_DEV):
                 place = target * PAIR_DEV + slot
-                if term < 2:
-                    value = looks[2 * place + term]
-                else:
-                    value = looks[2 * pairs + pair_ref[term - 2, owner_ref[place]]]
+                value = looks[2 * place + term]
                 turned = pltpu.roll(value, 4, 0)
                 if slot < 2:
                     value = jnp.where(group_zero, value, turned)
@@ -242,7 +290,7 @@
                 held = jnp.where(here, value, held)
             message[k, 8 * term : 8 * term + 8] = held
         for side in range(2):
-            edges[k, side] = message[k, pl.ds(3 * side, 8, stride=4)]
+            edges[k, side] = message[k, pl.ds(3 * side, 4, stride=4)]
         if own:
             got[me] = message[k]
         else:
@@ -266,8 +314,60 @@
             copy.start()
             back.append(copy)
 
-    for copy in started[max(parts - window, 0) * len(others) :]:
-        copy.wait_send()
+    for k, target in enumerate(targets):
+        if k < wide - 1:
+            pltpu.make_async_remote_copy(
+                src_ref=own_power,
+                dst_ref=power.at[pl.ds(2 * target, 2)],
+                send_sem=power_send.at[k],
+                recv_sem=power_recv.at[target],
+                device_id={"wide": target},
+            ).wait_recv()
+        for side in range(2):
+            pltpu.make_async_remote_copy(
+                src_ref=own_rims.at[side],
+                dst_ref=rims.at[side, pl.ds(2 * target, 2)],
+                send_sem=rim_send.at[side, k],
+                recv_sem=rim_recv.at[side, target],
+                device_id={"wide": target, "narrow": (above, below)[side]},
+            ).wait_recv()
+
+    columns = wide * 64
+    place = lax.broadcasted_iota(jnp.int32, (4, columns), 1)
+
+    def box(field):
+        rows = grown[field][0:4] + grown[field][1:5] + grown[field][2:6]
+        before = jnp.where(place == 0, 0.0, pltpu.roll(rows, 1, 1))
+        after = jnp.where(place == columns - 1, 0.0, pltpu.roll(rows, columns - 1, 1))
+        return before + rows + after
+
+    spare = jnp.zeros((2, LANES), jnp.float32)
+    for slot in range(PAIR_DEV):
+        chosen = owner_ref[me * PAIR_DEV + slot]
+        for term in range(2):
+            date = pair_ref[term, chosen]
+            value = power[date]
+            top = jnp.where(row == 0, 0.0, rims[1, date])
+            bottom = jnp.where(row == narrow - 1, 0.0, rims[0, date])
+            groups = [
+                jnp.concatenate(
+                    [top[g : g + 1], value[4 * g : 4 * g + 4], bottom[g : g + 1], spare], axis=0
+                )
+                for g in range(2)
+            ]
+            for tile in range(2):
+                held = None
+                for index in range(4):
+                    e, g = index // 2, index % 2
+                    shift = 32 * (e + g - 2 * tile) % LANES
+                    moved = pltpu.roll(groups[g], shift, 1) if shift else groups[g]
+                    if held is None:
+                        held = moved
+                    else:
+                        held = jnp.where(lane // 32 == index, moved, held)
+                grown[2 + term, slot, :, tile * LANES : (tile + 1) * LANES] = held
+        below_line[slot] = jnp.sqrt(box((2, slot)) * box((3, slot)) + 1e-06)
+
     for k, target in enumerate(targets):
         if k < wide - 1:
             pltpu.make_async_remote_copy(
@@ -288,12 +388,13 @@
 
     def across(parts, parity):
         tiles = []
+        first = lax.broadcasted_iota(jnp.int32, parts[0].shape, 1) < 64
         for i in range(0, wide, 2):
             one, two = parts[i], parts[i + 1]
             if parity == 0:
-                tiles.append(jnp.where(left, one, pltpu.roll(two, 64, 1)))
+                tiles.append(jnp.where(first, one, pltpu.roll(two, 64, 1)))
             else:
-                tiles.append(jnp.where(left, pltpu.roll(one, 64, 1), two))
+                tiles.append(jnp.where(first, pltpu.roll(one, 64, 1), two))
         return jnp.concatenate(tiles, axis=1)
 
     for parity in range(2):
@@ -301,7 +402,7 @@
         bottom = across([got_edges[0, w] for w in range(wide)], parity)
         top = jnp.where(row == 0, 0.0, top)
         bottom = jnp.where(row == narrow - 1, 0.0, bottom)
-        for term in range(4):
+        for term in range(2):
             middle = across([got[w, 8 * term : 8 * term + 8] for w in range(wide)], parity)
             for upper in range(2):
                 slot = 2 * upper + parity
@@ -310,19 +411,12 @@
                 grown[term, slot, 1:5] = middle[4 * upper : 4 * upper + 4]
                 grown[term, slot, 5:6] = bottom[edge : edge + 1]
 
-    columns = wide * 64
-    place = lax.broadcasted_iota(jnp.int32, (4, columns), 1)
     for slot in range(PAIR_DEV):
-        boxed = []
-        for term in range(4):
-            rows = grown[term, slot, 0:4] + grown[term, slot, 1:5] + grown[term, slot, 2:6]
-            before = jnp.where(place == 0, 0.0, pltpu.roll(rows, 1, 1))
-            after = jnp.where(place == columns - 1, 0.0, pltpu.roll(rows, columns - 1, 1))
-            boxed.append(before + rows + after)
-            if term < 2:
-                inter_ref[term, slot] = grown[term, slot, 1:5] / (ML_ROWS * ML_COLS)
+        boxed = [box((term, slot)) for term in range(2)]
+        for term in range(2):
+            inter_ref[term, slot] = grown[term, slot, 1:5] / (ML_ROWS * ML_COLS)
         magnitude = jnp.sqrt(boxed[0] * boxed[0] + boxed[1] * boxed[1])
-        coh_ref[slot] = magnitude / jnp.sqrt(boxed[2] * boxed[3] + 1e-06)
+        coh_ref[slot] = magnitude / below_line[slot]
 
     for copy in back:
         copy.wait_send()
@@ -350,14 +444,23 @@
     ]
     scratch += [
         pltpu.VMEM((2 * blocks, 8, LANES), f32),
-        pltpu.VMEM((wide, 32, LANES), f32),
-        pltpu.VMEM((wide, 2, 8, LANES), f32),
-        pltpu.VMEM((wide, 32, LANES), f32),
-        pltpu.VMEM((2, wide, 8, LANES), f32),
+        pltpu.VMEM((wide, 16, LANES), f32),
+        pltpu.VMEM((wide, 2, 4, LANES), f32),
+        pltpu.VMEM((wide, 16, LANES), f32),
+        pltpu.VMEM((2, wide, 4, LANES), f32),
+        pltpu.VMEM((2, 8, LANES), f32),
+        pltpu.VMEM((2, 2, 2, LANES), f32),
+        pltpu.VMEM((dates, 8, LANES), f32),
+        pltpu.VMEM((2, dates, 2, LANES), f32),
         pltpu.VMEM((4, PAIR_DEV, 8, wide * 64), f32),
+        pltpu.VMEM((PAIR_DEV, 4, wide * 64), f32),
         pltpu.SemaphoreType.DMA((wide,)),
         pltpu.SemaphoreType.DMA((len(widths), wide - 1)),
         pltpu.SemaphoreType.DMA((len(widths), wide)),
+        pltpu.SemaphoreType.DMA((wide,)),
+        pltpu.SemaphoreType.DMA((wide,)),
+        pltpu.SemaphoreType.DMA((2, wide)),
+        pltpu.SemaphoreType.DMA((2, wide)),
         pltpu.SemaphoreType.DMA((wide,)),
         pltpu.SemaphoreType.DMA((wide,)),
         pltpu.SemaphoreType.DMA((2, wide)),
@@ -366,7 +469,7 @@
     look_rows = slc.shape[2] // ML_ROWS
     look_columns = columns // ML_COLS
     return pl.pallas_call(
-        functools.partial(exchange_kernel, wide, narrow, half, widths, WINDOW),
+        functools.partial(exchange_kernel, wide, narrow, half, widths),
         out_shape=(
             pltpu.VMEM((2, PAIR_DEV, look_rows, look_columns), f32),
             pltpu.VMEM((PAIR_DEV, look_rows, look_columns), f32),
@@ -391,7 +494,7 @@
     def on_device(slc, pair_list, owner):
         wide, narrow = mesh.shape["wide"], mesh.shape["narrow"]
         tiled = slc.shape[3] == wide * 2 * ML_COLS * 32
-        if tiled and narrow > 2 and wide % 2 == 0 and slc.shape[1:3] == (2, 4 * ML_ROWS):
+        if tiled and narrow > 2 and wide == 4 and slc.shape[1:3] == (2, 4 * ML_ROWS):
             return exchanged(slc, pair_list, owner)
         return gathered(slc, pair_list, owner)
 

time: 33 us -> 32.8 us (level)
  no operation moved by 1% of the time
where the time goes in v3:
time: 32.8 us; the launch traced here: 32.6 us
  Pallas kernels  30.8 us (94%)
  local copies, waits for them, and re-layouts  1.22 us (4%)
  between operations  0.64 us (2%)
    pallas_call x1, Pallas kernels, exchanged(): pl.pallas_call(functools.partial(exchange_kernel, wide, narrow, half, wid...  30.8 us
    unnamed x2, local copies, waits for them, and re-layouts  1.22 us

profile of v3, /device:TPU:0, one launch (start us, length us, event | category | flops | bytes accessed | tf_op | source)
XLA Modules:
  0.0 32.6 jit_solution(15360186923028239674)
XLA Ops:
  0.6 30.8 %shard_map.50 = (f32[2,4,4,256]{3,2,1,0:T(4,128)S(1)}, f32[4,4,256]{2,1,0:T(4,128)S(1)}) custom-call(s32[2,16]{1,0:T(2,128)} %bitcast.3, s32[16]{0:T(128)} %owner_ref.1, bf16[2,20,2,5120]{3,2,1,0:T(2,128)(2,1)} %bitcast.2), custom_call_target="tpu_custom_call" | custom-call | tf_op jit(solution)/shard_map/pallas_call | solution.py:471
  31.4 0.6 %copy.7 = f32[2,4,4,256]{3,2,1,0:T(4,128)} copy(f32[2,4,4,256]{3,2,1,0:T(4,128)S(1)} %get-tuple-element.2) | data formatting | bytes 65536
  32.0 0.6 %copy.8 = f32[4,4,256]{2,1,0:T(4,128)} copy(f32[4,4,256]{2,1,0:T(4,128)S(1)} %get-tuple-element.3) | data formatting | bytes 32768

commit v4 on v3

--- a/solution.py
+++ b/solution.py
@@ -60,7 +60,7 @@
 
 
 LANES = 128
-PART = 256
+PART = 128
 
 
 def split_terms(value):

time: 32.8 us -> 32.7 us (level)
  no operation moved by 1% of the time
where the time goes in v4:
time: 32.7 us; the launch traced here: 32.5 us
  Pallas kernels  30.6 us (94%)
  local copies, waits for them, and re-layouts  1.22 us (4%)
  between operations  0.64 us (2%)
    pallas_call x1, Pallas kernels, exchanged(): pl.pallas_call(functools.partial(exchange_kernel, wide, narrow, half, wid...  30.6 us
    unnamed x2, local copies, waits for them, and re-layouts  1.22 us

profile of v4, /device:TPU:0, one launch (start us, length us, event | category | flops | bytes accessed | tf_op | source)
XLA Modules:
  0.0 32.5 jit_solution(9680012783667908678)
XLA Ops:
  0.6 30.6 %shard_map.50 = (f32[2,4,4,256]{3,2,1,0:T(4,128)S(1)}, f32[4,4,256]{2,1,0:T(4,128)S(1)}) custom-call(s32[2,16]{1,0:T(2,128)} %bitcast.3, s32[16]{0:T(128)} %owner_ref.1, bf16[2,20,2,5120]{3,2,1,0:T(2,128)(2,1)} %bitcast.2), custom_call_target="tpu_custom_call" | custom-call | tf_op jit(solution)/shard_map/pallas_call | solution.py:471
  31.3 0.6 %copy.7 = f32[2,4,4,256]{3,2,1,0:T(4,128)} copy(f32[2,4,4,256]{3,2,1,0:T(4,128)S(1)} %get-tuple-element.2) | data formatting | bytes 65536
  31.9 0.6 %copy.8 = f32[4,4,256]{2,1,0:T(4,128)} copy(f32[4,4,256]{2,1,0:T(4,128)S(1)} %get-tuple-element.3) | data formatting | bytes 32768
